TPU v7x, 32 devices: a whole 2x2x4 slice. The times are simulated.
32 devices in a mesh: grp: 2 (over x), ep: 16 (over z, y, core).
Axes of the slice: x: 2, y: 2, z: 4, core: 2. Of those that a mesh axis runs over, the one named last changes fastest.
Arguments:
- states: bfloat16 [2, 1280, 2048], P(None, ('grp', 'ep')), may hold values from -6 to 6
- route_ids: int32 [2, 1280, 8], P(None, ('grp', 'ep')), may hold values from 0 to 15, all different within a row; in each aligned block of 40 rows (0 to 39, 40 to 79, ..., all dimensions but the last counted through in order) at most 30 rows name the same one
- route_gates: float32 [2, 1280, 8], P(None, ('grp', 'ep')), may hold values from 0.02 to 0.3
- moe_gain: float32 [2048], replicated, may hold values from 0.25 to 1.75
- final_gain: float32 [2048], replicated, may hold values from 0.25 to 1.75
- gate_proj: bfloat16 [16, 2048, 512], P('ep', 'grp'), may hold values from -0.125 to 0.125
- up_proj: bfloat16 [16, 2048, 512], P('ep', 'grp'), may hold values from -0.125 to 0.125
- down_proj: bfloat16 [16, 512, 2048], P('ep', 'grp'), may hold values from -0.25 to 0.25
- old_slots: int32 [16], replicated, may hold values from 0 to 15, each once
- new_slots: int32 [16], replicated, may hold values from 0 to 15, each once
- req_lengths: int32 [2, 2, 4], P(None, 'grp'), may hold values from 1 to 320, 640 in all within a row
- head_proj: bfloat16 [2048, 49152], P(None, ('grp', 'ep')), may hold values from -14 to 14
Outputs:
- mixed: bfloat16 [2, 1280, 2048], P(None, ('grp', 'ep'))
- moved_gate: bfloat16 [16, 2048, 512], P('ep', 'grp')
- moved_up: bfloat16 [16, 2048, 512], P('ep', 'grp')
- moved_down: bfloat16 [16, 512, 2048], P('ep', 'grp')
- log_probs: float32 [2, 8, 49152], P(None, None, ('grp', 'ep'))
Inputs may be any that keep to these rules, and one draw needn't show every extreme that they name: `route_ids`: in each aligned block of 40 rows (the rows of one device in one batch) no expert is named by more than 30 rows, a bound that some block reaches; the 8 ids of a row differ. `old_slots`: each expert once. `new_slots`: each expert once. `req_lengths`: the 4 lengths of a group in a batch sum to 640, and the largest is 320.
All inputs are finite; a program needn't handle non-finite values.
Results may differ from a plain program's by a relative error of at most 0.0035.
Values may be sent and summed in bfloat16 or wider, within the bound.
A program may use at most 128 MiB of HBM per device.

v0:
```python
import jax
import jax.numpy as jnp
from jax import lax
from jax.sharding import PartitionSpec as P


def normalize(rows, gain):
    scale = lax.rsqrt(jnp.mean(rows * rows, axis=-1, keepdims=True) + 1e-06)
    return (rows * scale * gain).astype(jnp.bfloat16)


def owner_table(placement):
    ident = jnp.arange(placement.shape[0], dtype=jnp.int32)
    hits = placement[None, :] == ident[:, None]
    return jnp.sum(jnp.where(hits, ident[None, :], 0), axis=1)


def reorder_blocks(weights, source, n_dest):
    shape = weights.shape
    blocks = weights.reshape(shape[0], shape[1], n_dest, shape[2] // n_dest)
    return jnp.take(blocks, source, axis=2).reshape(shape)


def build_sends(normed, expert_ids, owner, n_dest, capacity):
    tok_rows, top_count = expert_ids.shape
    experts_all = owner.shape[0]
    expert_hits = expert_ids[:, :, None] == jnp.arange(experts_all, dtype=jnp.int32)[None, None, :]
    destination = jnp.sum(jnp.where(expert_hits, owner[None, None, :], 0), axis=2)
    flat_dest = destination.reshape(-1)
    dest_hits = (flat_dest[:, None] == jnp.arange(n_dest, dtype=jnp.int32)[None, :]).astype(
        jnp.int32
    )
    earlier = jnp.cumsum(dest_hits, axis=0) - dest_hits
    position = jnp.sum(earlier * dest_hits, axis=1)
    slot_index = (flat_dest * capacity + position).reshape(tok_rows, top_count)
    slot_hits = (
        slot_index[:, :, None] == jnp.arange(n_dest * capacity, dtype=jnp.int32)[None, None, :]
    )
    selector = jnp.sum(slot_hits.astype(jnp.float32), axis=1).astype(jnp.bfloat16)
    sends = jnp.einsum("ts,td->sd", selector, normed, preferred_element_type=jnp.float32).astype(
        jnp.bfloat16
    )
    return (sends.reshape(n_dest, capacity, normed.shape[1]), slot_index)


def expert_block(rows, shards):
    gate_part, up_part, down_part = shards
    columns = rows
    gate_vals = jnp.dot(
        columns,
        lax.all_gather(gate_part, "grp", axis=1, tiled=True)[0],
        preferred_element_type=jnp.float32,
    )
    up_vals = jnp.dot(
        columns,
        lax.all_gather(up_part, "grp", axis=1, tiled=True)[0],
        preferred_element_type=jnp.float32,
    )
    hidden = (jax.nn.silu(gate_vals) * up_vals).astype(jnp.bfloat16)
    columns = hidden
    outputs = jnp.dot(
        columns,
        lax.all_gather(down_part, "grp", axis=1, tiled=True)[0],
        preferred_element_type=jnp.float32,
    )
    return outputs.astype(jnp.bfloat16)


def combine_rows(residual_rows, gates, returned_rows, slot_index):
    picked = returned_rows[slot_index].astype(jnp.float32)
    return (residual_rows + jnp.sum(gates[:, :, None] * picked, axis=1)).astype(jnp.bfloat16)


def per_device(
    states,
    route_ids,
    route_gates,
    moe_gain,
    final_gain,
    gate_proj,
    up_proj,
    down_proj,
    old_slots,
    new_slots,
    req_lengths,
    head_proj,
):
    n_dest = lax.axis_size("ep")
    column = lax.axis_index("ep")
    tok_rows = states.shape[1]
    width = states.shape[2]
    top_count = route_ids.shape[2]
    experts_all = old_slots.shape[0]
    capacity = min(tok_rows, max(2, 3 * tok_rows * top_count // (2 * experts_all)))
    old_owner = owner_table(old_slots)
    new_owner = owner_table(new_slots)
    source = jnp.take(old_owner, new_slots)
    spread = (
        lax.all_to_all(gate_proj, "ep", split_axis=2, concat_axis=2, tiled=True),
        lax.all_to_all(up_proj, "ep", split_axis=2, concat_axis=2, tiled=True),
        lax.all_to_all(down_proj, "ep", split_axis=2, concat_axis=2, tiled=True),
    )
    gate_sorted = reorder_blocks(spread[0], source, n_dest)
    up_sorted = reorder_blocks(spread[1], source, n_dest)
    down_sorted = reorder_blocks(spread[2], source, n_dest)
    moved = (
        lax.all_to_all(gate_sorted, "ep", split_axis=2, concat_axis=2, tiled=True),
        lax.all_to_all(up_sorted, "ep", split_axis=2, concat_axis=2, tiled=True),
        lax.all_to_all(down_sorted, "ep", split_axis=2, concat_axis=2, tiled=True),
    )
    moved_gate, moved_up, moved_down = moved
    residual = states.astype(jnp.float32)
    normed = normalize(residual, moe_gain)
    outputs = []
    for batch_index, owner, shards in (
        (0, old_owner, (gate_proj, up_proj, down_proj)),
        (1, new_owner, (moved_gate, moved_up, moved_down)),
    ):
        sends, slot_index = build_sends(
            normed[batch_index], route_ids[batch_index], owner, n_dest, capacity
        )
        arrived = lax.all_to_all(sends, "ep", split_axis=0, concat_axis=0, tiled=True)
        results = expert_block(arrived.reshape(n_dest * capacity, width), shards)
        returned = lax.all_to_all(
            results.reshape(n_dest, capacity, width), "ep", split_axis=0, concat_axis=0, tiled=True
        )
        outputs.append(
            combine_rows(
                residual[batch_index],
                route_gates[batch_index],
                returned.reshape(n_dest * capacity, width),
                slot_index,
            )
        )
    mixed = jnp.stack(outputs)
    request_ends = jnp.cumsum(req_lengths[:, 0, :], axis=-1) - 1
    local_ends = request_ends - column * tok_rows
    picker = (
        local_ends[:, :, None] == jnp.arange(tok_rows, dtype=jnp.int32)[None, None, :]
    ).astype(jnp.bfloat16)
    tail_terms = jnp.einsum("brt,btd->brd", picker, mixed, preferred_element_type=jnp.float32)
    group_tails = lax.psum(tail_terms.astype(jnp.bfloat16), "ep")
    gathered = lax.all_gather(group_tails, "grp", axis=1, tiled=True)
    finals = normalize(gathered.astype(jnp.float32), final_gain)
    logits = jnp.dot(finals.reshape(-1, width), head_proj, preferred_element_type=jnp.float32)
    top_val = lax.pmax(jnp.max(logits, axis=1), ("grp", "ep"))
    totals = lax.psum(jnp.sum(jnp.exp(logits - top_val[:, None]), axis=1), ("grp", "ep"))
    log_probs = (logits - top_val[:, None] - jnp.log(totals)[:, None]).reshape(
        2, -1, logits.shape[1]
    )
    return (mixed, moved_gate, moved_up, moved_down, log_probs)


def solution(mesh):
    placed = (
        P(None, ("grp", "ep"), None),
        P(None, ("grp", "ep"), None),
        P(None, ("grp", "ep"), None),
        P(),
        P(),
        P("ep", "grp", None),
        P("ep", "grp", None),
        P("ep", "grp", None),
        P(),
        P(),
        P(None, "grp", None),
        P(None, ("grp", "ep")),
    )
    return jax.shard_map(
        per_device,
        mesh=mesh,
        in_specs=placed,
        out_specs=(
            P(None, ("grp", "ep"), None),
            P("ep", "grp", None),
            P("ep", "grp", None),
            P("ep", "grp", None),
            P(None, None, ("grp", "ep")),
        ),
        check_vma=False,
    )
```

profile of v0, /device:TPU:0, one launch (start us, length us, event | category | flops | bytes accessed | tf_op | source)
XLA Modules:
  0.0 611.8 jit_solution(1638913436100575654)
XLA Ops:
  7.2 4.7 copy.107
  12.4 7.8 %reduce.6 = bf16[512,1024]{1,0:T(8,128)(2,1)} reduce(bf16[512,1,1024]{2,1,0:T(2,128)(2,1)S(1)} %bitcast.152, bf16[]{:T(256)} %broadcast.285), dimensions={1}, to_apply=%bitcast.118.reduce_sub_computation | reduce | bytes 2097154
  20.2 2.7 reshape.355
  22.9 7.7 %all-to-all-start.3 = ((bf16[16,2,16384]{2,1,0:T(2,128)(2,1)}), bf16[16,2,16384]{2,1,0:T(2,128)(2,1)}, u32[]{:S(2)}, u32[]{:S(2)}) async-start(bf16[16,2,16384]{2,1,0:T(2,128)(2,1)} %reshape.355), calls=%async_computation.3 | async-start | bytes 2097152 | tf_op jit(solution)/shard_map/all_to_all | solution.py:99
  30.6 2.0 copy.110
  32.6 7.8 %reduce.7 = bf16[512,1024]{1,0:T(8,128)(2,1)} reduce(bf16[512,1,1024]{2,1,0:T(2,128)(2,1)S(1)} %bitcast.156, bf16[]{:T(256)} %broadcast.285), dimensions={1}, to_apply=%bitcast.114.reduce_sub_computation | reduce | bytes 2097154
  40.3 2.7 reshape.351
  43.0 10.5 %all-to-all-done.3 = bf16[16,2,16384]{2,1,0:T(2,128)(2,1)} async-done(((bf16[16,2,16384]{2,1,0:T(2,128)(2,1)}), bf16[16,2,16384]{2,1,0:T(2,128)(2,1)}, u32[]{:S(2)}, u32[]{:S(2)}) %all-to-all-start.3) | async-done | bytes 1048608 | tf_op jit(solution)/shard_map/all_to_all | solution.py:99
  53.5 6.9 %all-to-all-start.5 = ((bf16[16,2,16384]{2,1,0:T(2,128)(2,1)}), bf16[16,2,16384]{2,1,0:T(2,128)(2,1)}, u32[]{:S(2)}, u32[]{:S(2)}) async-start(bf16[16,2,16384]{2,1,0:T(2,128)(2,1)} %reshape.351), calls=%async_computation.5 | async-start | bytes 2097152 | tf_op jit(solution)/shard_map/all_to_all | solution.py:100
  61.0 1.7 copy.113
  62.7 10.6 %reduce.4 = bf16[2048,256]{1,0:T(8,128)(2,1)S(1)} reduce(bf16[2048,1,256]{2,1,0:T(2,128)(2,1)S(1)} %bitcast.157, bf16[]{:T(256)} %broadcast.285), dimensions={1}, to_apply=%bitcast.110.reduce_sub_computation | reduce | bytes 2097154
  74.4 9.0 %all-to-all-done.5 = bf16[16,2,16384]{2,1,0:T(2,128)(2,1)} async-done(((bf16[16,2,16384]{2,1,0:T(2,128)(2,1)}), bf16[16,2,16384]{2,1,0:T(2,128)(2,1)}, u32[]{:S(2)}, u32[]{:S(2)}) %all-to-all-start.5) | async-done | bytes 1048608 | tf_op jit(solution)/shard_map/all_to_all | solution.py:100
  83.5 7.3 %all-to-all-start.7 = ((bf16[16,2,16384]{2,1,0:T(2,128)(2,1)}), bf16[16,2,16384]{2,1,0:T(2,128)(2,1)S(1)}, u32[]{:S(2)}, u32[]{:S(2)}) async-start(bf16[16,2,16384]{2,1,0:T(2,128)(2,1)} %reshape.347), calls=%async_computation.7 | async-start | bytes 2097152 | tf_op jit(solution)/shard_map/all_to_all | solution.py:101
  94.3 1.6 reshape.258
  95.9 17.7 %all-to-all-done.7 = bf16[16,2,16384]{2,1,0:T(2,128)(2,1)S(1)} async-done(((bf16[16,2,16384]{2,1,0:T(2,128)(2,1)}), bf16[16,2,16384]{2,1,0:T(2,128)(2,1)S(1)}, u32[]{:S(2)}, u32[]{:S(2)}) %all-to-all-start.7) | async-done | bytes 1048608 | tf_op jit(solution)/shard_map/all_to_all | solution.py:101
  114.6 6.9 %all-to-all-start.2 = ((bf16[16,30,2048]{2,1,0:T(8,128)(2,1)}), bf16[16,30,2048]{2,1,0:T(8,128)(2,1)S(1)}, u32[]{:S(2)}, u32[]{:S(2)}) async-start(bf16[16,30,2048]{2,1,0:T(8,128)(2,1)} %reshape.258), calls=%async_computation.2 | async-start | bytes 4194304 | tf_op jit(solution)/shard_map/all_to_all | solution.py:122
  123.5 2.9 convolution_convert_fusion.3
  126.3 2.9 reshape.252
  129.2 33.4 %all-to-all-done.2 = bf16[16,30,2048]{2,1,0:T(8,128)(2,1)S(1)} async-done(((bf16[16,30,2048]{2,1,0:T(8,128)(2,1)}), bf16[16,30,2048]{2,1,0:T(8,128)(2,1)S(1)}, u32[]{:S(2)}, u32[]{:S(2)}) %all-to-all-start.2) | async-done | bytes 1966112 | tf_op jit(solution)/shard_map/all_to_all | solution.py:122
  164.0 11.3 %all-to-all-start = ((bf16[16,30,2048]{2,1,0:T(8,128)(2,1)}), bf16[16,30,2048]{2,1,0:T(8,128)(2,1)}, u32[]{:S(2)}, u32[]{:S(2)}) async-start(bf16[16,30,2048]{2,1,0:T(8,128)(2,1)} %reshape.252), calls=%async_computation | async-start | bytes 4194304 | tf_op jit(solution)/shard_map/all_to_all | solution.py:122
  177.4 4.3 reshape.356
  182.1 5.9 reshape.352
  188.0 2.1 copy.126
  191.6 1.6 copy.148
  193.2 7.8 %reduce.9 = bf16[512,1024]{1,0:T(8,128)(2,1)} reduce(bf16[512,1,1024]{2,1,0:T(2,128)(2,1)S(1)} %bitcast.154, bf16[]{:T(256)} %broadcast.285), dimensions={1}, to_apply=%bitcast.141.reduce_sub_computation | reduce | bytes 2097154
  201.0 2.6 reshape.357
  203.6 12.8 %all-to-all-done = bf16[16,30,2048]{2,1,0:T(8,128)(2,1)} async-done(((bf16[16,30,2048]{2,1,0:T(8,128)(2,1)}), bf16[16,30,2048]{2,1,0:T(8,128)(2,1)}, u32[]{:S(2)}, u32[]{:S(2)}) %all-to-all-start) | async-done | bytes 1966112 | tf_op jit(solution)/shard_map/all_to_all | solution.py:122
  216.4 11.3 %all-to-all-start.4 = ((bf16[16,2,16384]{2,1,0:T(2,128)(2,1)}), bf16[16,2,16384]{2,1,0:T(2,128)(2,1)}, u32[]{:S(2)}, u32[]{:S(2)}) async-start(bf16[16,2,16384]{2,1,0:T(2,128)(2,1)} %reshape.357), calls=%async_computation.4 | async-start | bytes 2097152 | tf_op jit(solution)/shard_map/all_to_all | solution.py:107
  228.4 1.6 copy.147
  230.0 6.8 %reduce.8 = bf16[512,1024]{1,0:T(8,128)(2,1)S(1)} reduce(bf16[512,1,1024]{2,1,0:T(2,128)(2,1)S(1)} %bitcast.155, bf16[]{:T(256)} %broadcast.285), dimensions={1}, to_apply=%bitcast.140.reduce_sub_computation | reduce | bytes 2097154
  236.8 1.6 reshape.353
  238.4 12.2 %all-to-all-done.4 = bf16[16,2,16384]{2,1,0:T(2,128)(2,1)} async-done(((bf16[16,2,16384]{2,1,0:T(2,128)(2,1)}), bf16[16,2,16384]{2,1,0:T(2,128)(2,1)}, u32[]{:S(2)}, u32[]{:S(2)}) %all-to-all-start.4) | async-done | bytes 1048608 | tf_op jit(solution)/shard_map/all_to_all | solution.py:107
  250.7 6.9 %all-to-all-start.6 = ((bf16[16,2,16384]{2,1,0:T(2,128)(2,1)}), bf16[16,2,16384]{2,1,0:T(2,128)(2,1)}, u32[]{:S(2)}, u32[]{:S(2)}) async-start(bf16[16,2,16384]{2,1,0:T(2,128)(2,1)} %reshape.353), calls=%async_computation.6 | async-start | bytes 2097152 | tf_op jit(solution)/shard_map/all_to_all | solution.py:108
  257.8 4.3 reshape.358
  262.2 4.2 copy.109
  270.3 11.7 %copy.146 = bf16[1,256,2048]{1,0,2:T(2,128)(2,1)S(1)} copy(bf16[1,256,2048]{1,2,0:T(8,128)(2,1)S(1)} %bitcast_select_fusion.2) | data formatting | bytes 2097152 | tf_op jit(solution)/shard_map/jit(_take)/select_n | solution.py:21
  282.0 10.6 %reduce.5 = bf16[2048,256]{1,0:T(8,128)(2,1)S(1)} reduce(bf16[2048,1,256]{2,1,0:T(2,128)(2,1)S(1)} %bitcast.153, bf16[]{:T(256)} %broadcast.285), dimensions={1}, to_apply=%bitcast.139.reduce_sub_computation | reduce | bytes 2097154
  293.7 6.0 all-to-all-start.8
  299.7 4.3 reshape.354
  304.1 4.2 copy.112
  308.3 1.8 reshape.253
  310.2 3.7 fusion.10
  313.9 6.1 convolution_convert_fusion.2
  320.0 2.8 reshape.254
  322.8 6.7 %all-to-all-start.1 = ((bf16[16,30,2048]{2,1,0:T(8,128)(2,1)}), bf16[16,30,2048]{2,1,0:T(8,128)(2,1)}, u32[]{:S(2)}, u32[]{:S(2)}) async-start(bf16[16,30,2048]{2,1,0:T(8,128)(2,1)} %reshape.254), calls=%async_computation.1 | async-start | bytes 4194304 | tf_op jit(solution)/shard_map/all_to_all | solution.py:124
  330.9 4.2 copy.117
  335.2 1.8 reshape.259
  337.0 2.8 fusion.5
  339.8 11.9 %all-gather.15.cloned.1.call-done = bf16[1,2048,512]{2,1,0:T(8,128)(2,1)} async-done(((bf16[1,1024,512]{2,1,0:T(8,128)(2,1)}), bf16[1,2048,512]{2,1,0:T(8,128)(2,1)}) %all-gather.15.cloned.1.call-update) | async-done | bytes 2097168 | tf_op jit(solution)/shard_map/all_gather | solution.py:56
  351.7 35.1 %all-gather.17.cloned.1.call-done = bf16[1,512,2048]{2,1,0:T(8,128)(2,1)} async-done(((bf16[1,256,2048]{2,1,0:T(8,128)(2,1)}), bf16[1,512,2048]{2,1,0:T(8,128)(2,1)}) %all-gather.17.cloned.1.call-update) | async-done | bytes 2097168 | tf_op jit(solution)/shard_map/all_gather | solution.py:63
  386.8 5.9 convolution_convert_fusion
  392.7 2.8 reshape.265
  395.5 5.8 all-to-all-start.9
  403.3 1.8 reshape.255
  405.1 2.4 gather_fusion
  407.6 2.0 fusion.1
  409.5 32.9 %all-to-all-done.9 = bf16[16,30,2048]{2,1,0:T(8,128)(2,1)} async-done(((bf16[16,30,2048]{2,1,0:T(8,128)(2,1)}), bf16[16,30,2048]{2,1,0:T(8,128)(2,1)}, u32[]{:S(2)}, u32[]{:S(2)}) %all-to-all-start.9) | async-done | bytes 1966112 | tf_op jit(solution)/shard_map/all_to_all | solution.py:124
  442.5 1.8 reshape.266
  444.3 2.4 gather_fusion.3
  449.4 67.3 %psum.14 = bf16[2,4,2048]{2,1,0:T(4,128)(2,1)S(1)} all-reduce(bf16[2,4,2048]{2,1,0:T(4,128)(2,1)S(1)} %convolution_convert_fusion.4), channel_id=1, replica_groups=mesh['grp'=2,'ep'=16] {'ep'}, use_global_device_ids=true, to_apply=%region_16.18 | all-reduce | flops 16384 | bytes 65536 | tf_op jit(solution)/shard_map/psum | solution.py:142
  516.7 4.6 all_gather.27
  521.4 3.9 fusion.50
  525.3 36.9 %pmax.7 = f32[16]{0:T(128)S(1)} all-reduce(f32[16]{0:T(128)S(1)} %get-tuple-element.41), channel_id=1, replica_groups=mesh['grp'=2,'ep'=16] {'grp','ep'}, use_global_device_ids=true, to_apply=%region_19.21 | all-reduce | flops 16 | bytes 128 | tf_op jit(solution)/shard_map/pmax | solution.py:146
  562.4 41.4 %psum.15 = f32[16]{0:T(128)S(1)} all-reduce(f32[16]{0:T(128)S(1)} %exponential_reduce_fusion), channel_id=1, replica_groups=mesh['grp'=2,'ep'=16] {'grp','ep'}, use_global_device_ids=true, to_apply=%region_21.23 | all-reduce | flops 16 | bytes 128 | tf_op jit(solution)/shard_map/psum | solution.py:147
  (135 shorter events, 26.9 us)
Async XLA Ops:
  20.2 10.4 %copy-start.2 = (bf16[1,1024,512]{2,1,0:T(8,128)(2,1)S(1)}, bf16[1,1024,512]{2,1,0:T(8,128)(2,1)}, u32[]{:S(2)}) copy-start(bf16[1,1024,512]{2,1,0:T(8,128)(2,1)} %param.20) | copy-start | bytes 3145732
  22.9 30.6 %all-to-all-start.3 = ((bf16[16,2,16384]{2,1,0:T(2,128)(2,1)}), bf16[16,2,16384]{2,1,0:T(2,128)(2,1)}, u32[]{:S(2)}, u32[]{:S(2)}) async-start(bf16[16,2,16384]{2,1,0:T(2,128)(2,1)} %reshape.355), calls=%async_computation.3 | async-start | bytes 2097152 | tf_op jit(solution)/shard_map/all_to_all | solution.py:99
  40.3 20.1 %copy-start.15 = (s32[16]{0:T(128)S(1)}, s32[16]{0:T(128)}, u32[]{:S(2)}) copy-start(s32[16]{0:T(128)} %param.22) | copy-start | bytes 196
  40.3 20.3 %copy-start.14 = (s32[16]{0:T(128)S(1)}, s32[16]{0:T(128)}, u32[]{:S(2)}) copy-start(s32[16]{0:T(128)} %param.23) | copy-start | bytes 196
  40.3 20.4 %copy-start.10 = (s32[2,40,8]{1,2,0:T(8,128)S(1)}, s32[2,40,8]{1,2,0:T(8,128)}, u32[]{:S(2)}) copy-start(s32[2,40,8]{1,2,0:T(8,128)} %param.15) | copy-start | bytes 7684
  40.3 20.7 %copy-start.1 = (bf16[1,256,2048]{2,1,0:T(8,128)(2,1)S(1)}, bf16[1,256,2048]{2,1,0:T(8,128)(2,1)}, u32[]{:S(2)}) copy-start(bf16[1,256,2048]{2,1,0:T(8,128)(2,1)} %param.21) | copy-start | bytes 3145732
  53.5 29.9 %all-to-all-start.5 = ((bf16[16,2,16384]{2,1,0:T(2,128)(2,1)}), bf16[16,2,16384]{2,1,0:T(2,128)(2,1)}, u32[]{:S(2)}, u32[]{:S(2)}) async-start(bf16[16,2,16384]{2,1,0:T(2,128)(2,1)} %reshape.351), calls=%async_computation.5 | async-start | bytes 2097152 | tf_op jit(solution)/shard_map/all_to_all | solution.py:100
  73.3 19.2 %copy-start.5 = (bf16[2,40,2048]{2,1,0:T(8,128)(2,1)S(1)}, bf16[2,40,2048]{2,1,0:T(8,128)(2,1)}, u32[]{:S(2)}) copy-start(bf16[2,40,2048]{2,1,0:T(8,128)(2,1)} %param.14) | copy-start | bytes 983044
  73.3 19.4 %copy-start.12 = (f32[2048]{0:T(1024)S(1)}, f32[2048]{0:T(1024)}, u32[]{:S(2)}) copy-start(f32[2048]{0:T(1024)} %param.17) | copy-start | bytes 24580
  83.5 30.2 %all-to-all-start.7 = ((bf16[16,2,16384]{2,1,0:T(2,128)(2,1)}), bf16[16,2,16384]{2,1,0:T(2,128)(2,1)S(1)}, u32[]{:S(2)}, u32[]{:S(2)}) async-start(bf16[16,2,16384]{2,1,0:T(2,128)(2,1)} %reshape.347), calls=%async_computation.7 | async-start | bytes 2097152 | tf_op jit(solution)/shard_map/all_to_all | solution.py:101
  92.8 0.7 copy-start.7
  113.6 1.0 copy-start.3
  114.6 48.0 %all-to-all-start.2 = ((bf16[16,30,2048]{2,1,0:T(8,128)(2,1)}), bf16[16,30,2048]{2,1,0:T(8,128)(2,1)S(1)}, u32[]{:S(2)}, u32[]{:S(2)}) async-start(bf16[16,30,2048]{2,1,0:T(8,128)(2,1)} %reshape.258), calls=%async_computation.2 | async-start | bytes 4194304 | tf_op jit(solution)/shard_map/all_to_all | solution.py:122
  162.6 1.4 copy-start
  164.0 52.4 %all-to-all-start = ((bf16[16,30,2048]{2,1,0:T(8,128)(2,1)}), bf16[16,30,2048]{2,1,0:T(8,128)(2,1)}, u32[]{:S(2)}, u32[]{:S(2)}) async-start(bf16[16,30,2048]{2,1,0:T(8,128)(2,1)} %reshape.252), calls=%async_computation | async-start | bytes 4194304 | tf_op jit(solution)/shard_map/all_to_all | solution.py:122
  175.2 134.9 %all-gather.7.cloned.1.call-start = ((), (), s32[]{:S(2)}) async-start(), calls=%async_computation.10 | async-start | bytes 3145728 | tf_op jit(solution)/shard_map/all_gather | solution.py:51
  176.0 137.9 %all-gather.11.cloned.1.call-start = ((), (), s32[]{:S(2)}) async-start(), calls=%async_computation.12 | async-start | bytes 3145728 | tf_op jit(solution)/shard_map/all_gather | solution.py:63
  216.4 34.3 %all-to-all-start.4 = ((bf16[16,2,16384]{2,1,0:T(2,128)(2,1)}), bf16[16,2,16384]{2,1,0:T(2,128)(2,1)}, u32[]{:S(2)}, u32[]{:S(2)}) async-start(bf16[16,2,16384]{2,1,0:T(2,128)(2,1)} %reshape.357), calls=%async_computation.4 | async-start | bytes 2097152 | tf_op jit(solution)/shard_map/all_to_all | solution.py:107
  227.7 86.2 %all-gather.9.cloned.1.call-start = ((), (), s32[]{:S(2)}) async-start(), calls=%async_computation.11 | async-start | bytes 3145728 | tf_op jit(solution)/shard_map/all_gather | solution.py:56
  250.7 43.1 %all-to-all-start.6 = ((bf16[16,2,16384]{2,1,0:T(2,128)(2,1)}), bf16[16,2,16384]{2,1,0:T(2,128)(2,1)}, u32[]{:S(2)}, u32[]{:S(2)}) async-start(bf16[16,2,16384]{2,1,0:T(2,128)(2,1)} %reshape.353), calls=%async_computation.6 | async-start | bytes 2097152 | tf_op jit(solution)/shard_map/all_to_all | solution.py:108
  257.6 79.4 %all-gather.13.cloned.1.call-start = ((), (), s32[]{:S(2)}) async-start(), calls=%async_computation.13 | async-start | bytes 3145728 | tf_op jit(solution)/shard_map/all_gather | solution.py:51
  262.2 4.3 copy-start.4
  293.7 29.1 %all-to-all-start.8 = ((bf16[16,2,16384]{2,1,0:T(2,128)(2,1)}), bf16[16,2,16384]{2,1,0:T(2,128)(2,1)S(1)}, u32[]{:S(2)}, u32[]{:S(2)}) async-start(bf16[16,2,16384]{2,1,0:T(2,128)(2,1)} %reshape.349), calls=%async_computation.8 | async-start | bytes 2097152 | tf_op jit(solution)/shard_map/all_to_all | solution.py:109
  299.7 52.0 %all-gather.15.cloned.1.call-start = ((), (), s32[]{:S(2)}) async-start(), calls=%async_computation.14 | async-start | bytes 3145728 | tf_op jit(solution)/shard_map/all_gather | solution.py:56
  322.8 72.7 %all-to-all-start.1 = ((bf16[16,30,2048]{2,1,0:T(8,128)(2,1)}), bf16[16,30,2048]{2,1,0:T(8,128)(2,1)}, u32[]{:S(2)}, u32[]{:S(2)}) async-start(bf16[16,30,2048]{2,1,0:T(8,128)(2,1)} %reshape.254), calls=%async_computation.1 | async-start | bytes 4194304 | tf_op jit(solution)/shard_map/all_to_all | solution.py:124
  329.6 57.2 %all-gather.17.cloned.1.call-start = ((), (), s32[]{:S(2)}) async-start(), calls=%async_computation.15 | async-start | bytes 3145728 | tf_op jit(solution)/shard_map/all_gather | solution.py:63
  395.5 7.2 %copy-start.11 = (f32[2,40,8]{1,2,0:T(8,128)S(1)}, f32[2,40,8]{1,2,0:T(8,128)}, u32[]{:S(2)}) copy-start(f32[2,40,8]{1,2,0:T(8,128)} %param.16) | copy-start | bytes 7684
  395.5 7.6 %copy-start.13 = (s32[2,1,4]{2,1,0:T(1,128)S(1)}, s32[2,1,4]{2,1,0:T(1,128)}, u32[]{:S(2)}) copy-start(s32[2,1,4]{2,1,0:T(1,128)} %param.24) | copy-start | bytes 100
  395.5 47.0 %all-to-all-start.9 = ((bf16[16,30,2048]{2,1,0:T(8,128)(2,1)}), bf16[16,30,2048]{2,1,0:T(8,128)(2,1)}, u32[]{:S(2)}, u32[]{:S(2)}) async-start(bf16[16,30,2048]{2,1,0:T(8,128)(2,1)} %reshape.265), calls=%async_computation.9 | async-start | bytes 4194304 | tf_op jit(solution)/shard_map/all_to_all | solution.py:124
  446.7 1.3 copy-start.6
  446.7 74.6 %copy-start.9 = (f32[2048]{0:T(1024)S(1)}, f32[2048]{0:T(1024)}, u32[]{:S(2)}) copy-start(f32[2048]{0:T(1024)} %param.18) | copy-start | bytes 24580
  449.1 76.1 %copy-start.8 = (bf16[2,40,2048]{2,1,0:T(8,128)(2,1)}, bf16[2,40,2048]{2,1,0:T(8,128)(2,1)S(1)}, u32[]{:S(2)}) copy-start(bf16[2,40,2048]{2,1,0:T(8,128)(2,1)S(1)} %pad_maximum_fusion) | copy-start | bytes 983044
Sparse Core Ops, SparseCore 0:
  177.6 34.3 all-gather.6
  213.6 33.1 all-gather.10
  248.3 33.1 all-gather.8
  283.4 33.1 all-gather.12
  318.5 33.1 all-gather.14
  353.6 33.1 all-gather.16
where the time goes:
time: 619 us; the launch traced here: 612 us
  waiting for transfers between devices  178 us (29%)
  blocking collectives  150 us (24%)
  local copies, waits for them, and re-layouts  103 us (17%)
  starting transfers between devices  77.6 us (13%)
  other arithmetic  61.8 us (10%)
  matrix products  26.1 us (4%)
  between operations  15.2 us (2%)
    psum x1, blocking collectives, per_device(): group_tails = lax.psum(tail_terms.astype(jnp.bfloat16), 'ep')  67.3 us
    unnamed x6, other arithmetic  51.2 us
    unnamed x51, local copies, waits for them, and re-layouts  47.4 us
    all_to_all x2, waiting for transfers between devices, per_device(): lax.all_to_all(sends, 'ep', split_axis=0, concat_axis=0, tiled=True)  46.2 us
    psum x1, blocking collectives, per_device(): lax.psum(jnp.sum(jnp.exp(logits - top_val[:, None]), axis=1), ('grp', 'ep'))  41.4 us
    pmax x1, blocking collectives, per_device(): top_val = lax.pmax(jnp.max(logits, axis=1), ('grp', 'ep'))  36.9 us
    all_gather x2, waiting for transfers between devices, expert_block(): lax.all_gather(down_part, 'grp', axis=1, tiled=True)[0]  35.1 us
    all_to_all x2, waiting for transfers between devices, per_device(): lax.all_to_all(results.reshape(n_dest, capacity, width), 'ep', split_axis...  32.9 us
  transfers between devices with their start and end apart: 16, of which 9 were waited for; matrix products, arithmetic and copies ran while one was open for 26% of the time, Pallas kernels for 0%

commit v1 on v0

--- a/solution.py
+++ b/solution.py
@@ -2,6 +2,16 @@
 import jax.numpy as jnp
 from jax import lax
 from jax.sharding import PartitionSpec as P
+
+name_series = lambda x_part, comm_axis, pos_dim, dimension_no: jnp.concatenate(
+    lax.all_to_all(
+        jnp.stack(jnp.split(x_part, lax.axis_size(comm_axis), pos_dim)),
+        axis_name=comm_axis,
+        split_axis=0,
+        concat_axis=0,
+    ),
+    axis=dimension_no,
+)
 
 
 def normalize(rows, gain):
@@ -104,7 +114,7 @@
     up_sorted = reorder_blocks(spread[1], source, n_dest)
     down_sorted = reorder_blocks(spread[2], source, n_dest)
     moved = (
-        lax.all_to_all(gate_sorted, "ep", split_axis=2, concat_axis=2, tiled=True),
+        name_series(gate_sorted, "ep", 2, dimension_no=2),
         lax.all_to_all(up_sorted, "ep", split_axis=2, concat_axis=2, tiled=True),
         lax.all_to_all(down_sorted, "ep", split_axis=2, concat_axis=2, tiled=True),
     )

time: 619 us -> 602 us (0.973)
  waiting for transfers between devices: 178 us -> 168 us
    all_gather x2, waiting for transfers between devices: 11.9 us -> 3.3 us  [expert_block(): lax.all_gather(up_part, 'grp', axis=1, tiled=True)[0]]
    unnamed x6 -> x5, other arithmetic: 51.2 us -> 43.5 us
    unnamed x51 -> x65, local copies, waits for them, and re-layouts: 47.4 us -> 52.1 us
where the time goes in v1:
time: 602 us; the launch traced here: 595 us
  waiting for transfers between devices  168 us (28%)
  blocking collectives  150 us (25%)
  local copies, waits for them, and re-layouts  103 us (17%)
  starting transfers between devices  76.9 us (13%)
  other arithmetic  55.7 us (9%)
  matrix products  26.1 us (4%)
  between operations  14.9 us (2%)
    psum x1, blocking collectives, per_device(): group_tails = lax.psum(tail_terms.astype(jnp.bfloat16), 'ep')  67.3 us
    unnamed x65, local copies, waits for them, and re-layouts  52.1 us
    all_to_all x2, waiting for transfers between devices, per_device(): lax.all_to_all(sends, 'ep', split_axis=0, concat_axis=0, tiled=True)  47.4 us
    unnamed x5, other arithmetic  43.5 us
    psum x1, blocking collectives, per_device(): lax.psum(jnp.sum(jnp.exp(logits - top_val[:, None]), axis=1), ('grp', 'ep'))  41.4 us
    pmax x1, blocking collectives, per_device(): top_val = lax.pmax(jnp.max(logits, axis=1), ('grp', 'ep'))  36.9 us
    all_gather x2, waiting for transfers between devices, expert_block(): lax.all_gather(down_part, 'grp', axis=1, tiled=True)[0]  35.1 us
    all_to_all x2, waiting for transfers between devices, per_device(): lax.all_to_all(results.reshape(n_dest, capacity, width), 'ep', split_axis...  33 us
  transfers between devices with their start and end apart: 16, of which 9 were waited for; matrix products, arithmetic and copies ran while one was open for 26% of the time, Pallas kernels for 0%

profile of v1, /device:TPU:0, one launch (start us, length us, event | category | flops | bytes accessed | tf_op | source)
XLA Modules:
  0.0 594.6 jit_solution(2639254218357375186)
XLA Ops:
  7.2 4.7 copy.119
  12.4 7.8 %reduce.6 = bf16[512,1024]{1,0:T(8,128)(2,1)} reduce(bf16[512,1,1024]{2,1,0:T(2,128)(2,1)S(1)} %bitcast.216, bf16[]{:T(256)} %broadcast.285), dimensions={1}, to_apply=%bitcast.185.reduce_sub_computation | reduce | bytes 2097154
  20.2 2.7 reshape.363
  22.9 7.6 %all-to-all-start.3 = ((bf16[16,2,16384]{2,1,0:T(2,128)(2,1)}), bf16[16,2,16384]{2,1,0:T(2,128)(2,1)}, u32[]{:S(2)}, u32[]{:S(2)}) async-start(bf16[16,2,16384]{2,1,0:T(2,128)(2,1)} %reshape.363), calls=%async_computation.3 | async-start | bytes 2097152 | tf_op jit(solution)/shard_map/all_to_all | solution.py:109
  30.5 2.0 copy.120
  32.5 6.8 %reduce.7 = bf16[512,1024]{1,0:T(8,128)(2,1)S(1)} reduce(bf16[512,1,1024]{2,1,0:T(2,128)(2,1)S(1)} %bitcast.219, bf16[]{:T(256)} %broadcast.285), dimensions={1}, to_apply=%bitcast.181.reduce_sub_computation | reduce | bytes 2097154
  39.3 1.6 reshape.359
  40.9 12.6 %all-to-all-done.3 = bf16[16,2,16384]{2,1,0:T(2,128)(2,1)} async-done(((bf16[16,2,16384]{2,1,0:T(2,128)(2,1)}), bf16[16,2,16384]{2,1,0:T(2,128)(2,1)}, u32[]{:S(2)}, u32[]{:S(2)}) %all-to-all-start.3) | async-done | bytes 1048608 | tf_op jit(solution)/shard_map/all_to_all | solution.py:109
  53.5 6.9 %all-to-all-start.5 = ((bf16[16,2,16384]{2,1,0:T(2,128)(2,1)}), bf16[16,2,16384]{2,1,0:T(2,128)(2,1)}, u32[]{:S(2)}, u32[]{:S(2)}) async-start(bf16[16,2,16384]{2,1,0:T(2,128)(2,1)} %reshape.359), calls=%async_computation.5 | async-start | bytes 2097152 | tf_op jit(solution)/shard_map/all_to_all | solution.py:110
  61.7 1.7 copy.123
  63.4 10.6 %reduce.4 = bf16[2048,256]{1,0:T(8,128)(2,1)S(1)} reduce(bf16[2048,1,256]{2,1,0:T(2,128)(2,1)S(1)} %bitcast.220, bf16[]{:T(256)} %broadcast.285), dimensions={1}, to_apply=%bitcast.177.reduce_sub_computation | reduce | bytes 2097154
  75.1 8.3 %all-to-all-done.5 = bf16[16,2,16384]{2,1,0:T(2,128)(2,1)} async-done(((bf16[16,2,16384]{2,1,0:T(2,128)(2,1)}), bf16[16,2,16384]{2,1,0:T(2,128)(2,1)}, u32[]{:S(2)}, u32[]{:S(2)}) %all-to-all-start.5) | async-done | bytes 1048608 | tf_op jit(solution)/shard_map/all_to_all | solution.py:110
  83.4 7.3 %all-to-all-start.7 = ((bf16[16,2,16384]{2,1,0:T(2,128)(2,1)}), bf16[16,2,16384]{2,1,0:T(2,128)(2,1)S(1)}, u32[]{:S(2)}, u32[]{:S(2)}) async-start(bf16[16,2,16384]{2,1,0:T(2,128)(2,1)} %reshape.355), calls=%async_computation.7 | async-start | bytes 2097152 | tf_op jit(solution)/shard_map/all_to_all | solution.py:111
  93.5 1.6 convolution_convert_fusion.1
  95.1 1.6 reshape.264
  96.8 16.8 %all-to-all-done.7 = bf16[16,2,16384]{2,1,0:T(2,128)(2,1)S(1)} async-done(((bf16[16,2,16384]{2,1,0:T(2,128)(2,1)}), bf16[16,2,16384]{2,1,0:T(2,128)(2,1)S(1)}, u32[]{:S(2)}, u32[]{:S(2)}) %all-to-all-start.7) | async-done | bytes 1048608 | tf_op jit(solution)/shard_map/all_to_all | solution.py:111
  114.6 6.9 %all-to-all-start.2 = ((bf16[16,30,2048]{2,1,0:T(8,128)(2,1)}), bf16[16,30,2048]{2,1,0:T(8,128)(2,1)}, u32[]{:S(2)}, u32[]{:S(2)}) async-start(bf16[16,30,2048]{2,1,0:T(8,128)(2,1)} %reshape.264), calls=%async_computation.2 | async-start | bytes 4194304 | tf_op jit(solution)/shard_map/all_to_all | solution.py:132
  124.9 1.6 convolution_convert_fusion.3
  126.5 1.7 reshape.258
  128.2 5.9 reshape.364
  134.1 2.1 copy.135
  136.2 5.8 reshape.360
  142.0 2.0 copy.136
  145.3 17.4 %all-to-all-done.2 = bf16[16,30,2048]{2,1,0:T(8,128)(2,1)} async-done(((bf16[16,30,2048]{2,1,0:T(8,128)(2,1)}), bf16[16,30,2048]{2,1,0:T(8,128)(2,1)}, u32[]{:S(2)}, u32[]{:S(2)}) %all-to-all-start.2) | async-done | bytes 1966112 | tf_op jit(solution)/shard_map/all_to_all | solution.py:132
  162.7 11.3 %all-to-all-start = ((bf16[16,30,2048]{2,1,0:T(8,128)(2,1)}), bf16[16,30,2048]{2,1,0:T(8,128)(2,1)}, u32[]{:S(2)}, u32[]{:S(2)}) async-start(bf16[16,30,2048]{2,1,0:T(8,128)(2,1)} %reshape.258), calls=%async_computation | async-start | bytes 4194304 | tf_op jit(solution)/shard_map/all_to_all | solution.py:132
  173.9 1.2 bitcast_select_fusion.1
  185.1 30.0 %all-to-all-done = bf16[16,30,2048]{2,1,0:T(8,128)(2,1)} async-done(((bf16[16,30,2048]{2,1,0:T(8,128)(2,1)}), bf16[16,30,2048]{2,1,0:T(8,128)(2,1)}, u32[]{:S(2)}, u32[]{:S(2)}) %all-to-all-start) | async-done | bytes 1966112 | tf_op jit(solution)/shard_map/all_to_all | solution.py:132
  215.1 11.2 %all-to-all-start.4 = ((bf16[16,1,1024,32]{2,3,1,0:T(8,128)(2,1)}), bf16[16,1,1024,32]{2,3,1,0:T(8,128)(2,1)S(1)}, u32[]{:S(2)}, u32[]{:S(2)}) async-start(bf16[16,1,1024,32]{2,3,1,0:T(8,128)(2,1)} %fusion.38), calls=%async_computation.4 | async-start | bytes 2097152 | tf_op jit(solution)/shard_map/all_to_all | solution.py:7
  227.1 2.8 copy.156
  229.9 7.8 %reduce.8 = bf16[512,1024]{1,0:T(8,128)(2,1)} reduce(bf16[512,1,1024]{2,1,0:T(2,128)(2,1)S(1)} %bitcast.218, bf16[]{:T(256)} %broadcast.285), dimensions={1}, to_apply=%bitcast.204.reduce_sub_computation | reduce | bytes 2097154
  237.7 2.6 reshape.361
  240.3 9.0 %all-to-all-done.4 = bf16[16,1,1024,32]{2,3,1,0:T(8,128)(2,1)S(1)} async-done(((bf16[16,1,1024,32]{2,3,1,0:T(8,128)(2,1)}), bf16[16,1,1024,32]{2,3,1,0:T(8,128)(2,1)S(1)}, u32[]{:S(2)}, u32[]{:S(2)}) %all-to-all-start.4) | async-done | bytes 1048608 | tf_op jit(solution)/shard_map/all_to_all | solution.py:7
  249.3 6.9 %all-to-all-start.6 = ((bf16[16,2,16384]{2,1,0:T(2,128)(2,1)}), bf16[16,2,16384]{2,1,0:T(2,128)(2,1)}, u32[]{:S(2)}, u32[]{:S(2)}) async-start(bf16[16,2,16384]{2,1,0:T(2,128)(2,1)} %reshape.361), calls=%async_computation.6 | async-start | bytes 2097152 | tf_op jit(solution)/shard_map/all_to_all | solution.py:118
  260.6 11.7 %copy.155 = bf16[1,256,2048]{1,0,2:T(2,128)(2,1)S(1)} copy(bf16[1,256,2048]{1,2,0:T(8,128)(2,1)S(1)} %bitcast_select_fusion.2) | data formatting | bytes 2097152 | tf_op jit(solution)/shard_map/jit(_take)/select_n | solution.py:31
  272.4 10.6 %reduce.5 = bf16[2048,256]{1,0:T(8,128)(2,1)S(1)} reduce(bf16[2048,1,256]{2,1,0:T(2,128)(2,1)S(1)} %bitcast.217, bf16[]{:T(256)} %broadcast.285), dimensions={1}, to_apply=%bitcast.203.reduce_sub_computation | reduce | bytes 2097154
  284.1 6.0 %all-to-all-start.8 = ((bf16[16,2,16384]{2,1,0:T(2,128)(2,1)}), bf16[16,2,16384]{2,1,0:T(2,128)(2,1)S(1)}, u32[]{:S(2)}, u32[]{:S(2)}) async-start(bf16[16,2,16384]{2,1,0:T(2,128)(2,1)} %reshape.357), calls=%async_computation.8 | async-start | bytes 2097152 | tf_op jit(solution)/shard_map/all_to_all | solution.py:119
  290.1 4.3 reshape.362
  294.4 4.2 copy.122
  298.7 1.8 reshape.259
  300.5 3.7 fusion.10
  304.2 6.4 %convolution_convert_fusion.2 = bf16[480,2048]{1,0:T(8,128)(2,1)} fusion(bf16[1,512,2048]{2,1,0:T(8,128)(2,1)} %all-gather.11.cloned.1.call-done, bf16[480,2048]{1,0:T(8,128)(2,1)S(1)} %reshape.259, bf16[1,2048,512]{2,1,0:T(8,128)(2,1)} %all-gather.9.cloned.1.call-done, f32[480,512]{1,0:T(8,128)} %fusion.10), kind=kOutput, calls=%fused_computation.8 | convolution fusion | flops 2015723520 | bytes 9109504 | tf_op jit(solution)/shard_map/dot_general | solution.py:71
  310.6 2.8 reshape.260
  313.4 6.5 %all-to-all-start.1 = ((bf16[16,30,2048]{2,1,0:T(8,128)(2,1)}), bf16[16,30,2048]{2,1,0:T(8,128)(2,1)}, u32[]{:S(2)}, u32[]{:S(2)}) async-start(bf16[16,30,2048]{2,1,0:T(8,128)(2,1)} %reshape.260), calls=%async_computation.1 | async-start | bytes 4194304 | tf_op jit(solution)/shard_map/all_to_all | solution.py:134
  321.0 4.2 copy.127
  325.3 1.8 reshape.265
  327.1 2.8 fusion.5
  329.9 3.3 all-gather.15.cloned.1.call-done
  333.2 35.1 %all-gather.17.cloned.1.call-done = bf16[1,512,2048]{2,1,0:T(8,128)(2,1)} async-done(((bf16[1,256,2048]{2,1,0:T(8,128)(2,1)}), bf16[1,512,2048]{2,1,0:T(8,128)(2,1)}) %all-gather.17.cloned.1.call-update) | async-done | bytes 2097168 | tf_op jit(solution)/shard_map/all_gather | solution.py:73
  368.4 5.9 convolution_convert_fusion
  374.2 2.8 reshape.273
  377.1 5.9 all-to-all-start.9
  384.9 1.8 reshape.261
  386.8 2.4 gather_fusion
  389.2 2.0 fusion.1
  391.2 33.0 %all-to-all-done.9 = bf16[16,30,2048]{2,1,0:T(8,128)(2,1)} async-done(((bf16[16,30,2048]{2,1,0:T(8,128)(2,1)}), bf16[16,30,2048]{2,1,0:T(8,128)(2,1)}, u32[]{:S(2)}, u32[]{:S(2)}) %all-to-all-start.9) | async-done | bytes 1966112 | tf_op jit(solution)/shard_map/all_to_all | solution.py:134
  424.1 1.8 reshape.274
  425.9 2.4 gather_fusion.3
  428.4 1.3 fusion
  431.0 67.3 %psum.14 = bf16[2,4,2048]{2,1,0:T(4,128)(2,1)S(1)} all-reduce(bf16[2,4,2048]{2,1,0:T(4,128)(2,1)S(1)} %convolution_convert_fusion.4), channel_id=1, replica_groups=mesh['grp'=2,'ep'=16] {'ep'}, use_global_device_ids=true, to_apply=%region_16.18 | all-reduce | flops 16384 | bytes 65536 | tf_op jit(solution)/shard_map/psum | solution.py:152
  498.3 4.6 all_gather.27
  503.1 4.0 fusion.66
  507.0 36.9 %pmax.7 = f32[16]{0:T(128)S(1)} all-reduce(f32[16]{0:T(128)S(1)} %get-tuple-element.41), channel_id=1, replica_groups=mesh['grp'=2,'ep'=16] {'grp','ep'}, use_global_device_ids=true, to_apply=%region_19.21 | all-reduce | flops 16 | bytes 128 | tf_op jit(solution)/shard_map/pmax | solution.py:156
  544.1 1.3 copy.132
  545.4 41.4 %psum.15 = f32[16]{0:T(128)S(1)} all-reduce(f32[16]{0:T(128)S(1)} %exponential_reduce_fusion), channel_id=1, replica_groups=mesh['grp'=2,'ep'=16] {'grp','ep'}, use_global_device_ids=true, to_apply=%region_21.23 | all-reduce | flops 16 | bytes 128 | tf_op jit(solution)/shard_map/psum | solution.py:157
  (147 shorter events, 32.9 us)
Async XLA Ops:
  20.2 10.3 %copy-start.3 = (bf16[1,1024,512]{2,1,0:T(8,128)(2,1)S(1)}, bf16[1,1024,512]{2,1,0:T(8,128)(2,1)}, u32[]{:S(2)}) copy-start(bf16[1,1024,512]{2,1,0:T(8,128)(2,1)} %param.20) | copy-start | bytes 3145732
  22.9 30.6 %all-to-all-start.3 = ((bf16[16,2,16384]{2,1,0:T(2,128)(2,1)}), bf16[16,2,16384]{2,1,0:T(2,128)(2,1)}, u32[]{:S(2)}, u32[]{:S(2)}) async-start(bf16[16,2,16384]{2,1,0:T(2,128)(2,1)} %reshape.363), calls=%async_computation.3 | async-start | bytes 2097152 | tf_op jit(solution)/shard_map/all_to_all | solution.py:109
  40.9 20.3 %copy-start.15 = (s32[16]{0:T(128)S(1)}, s32[16]{0:T(128)}, u32[]{:S(2)}) copy-start(s32[16]{0:T(128)} %param.22) | copy-start | bytes 196
  40.9 20.4 %copy-start.14 = (s32[16]{0:T(128)S(1)}, s32[16]{0:T(128)}, u32[]{:S(2)}) copy-start(s32[16]{0:T(128)} %param.23) | copy-start | bytes 196
  40.9 20.5 %copy-start.10 = (s32[2,40,8]{1,2,0:T(8,128)S(1)}, s32[2,40,8]{1,2,0:T(8,128)}, u32[]{:S(2)}) copy-start(s32[2,40,8]{1,2,0:T(8,128)} %param.15) | copy-start | bytes 7684
  40.9 20.8 %copy-start.2 = (bf16[1,256,2048]{2,1,0:T(8,128)(2,1)S(1)}, bf16[1,256,2048]{2,1,0:T(8,128)(2,1)}, u32[]{:S(2)}) copy-start(bf16[1,256,2048]{2,1,0:T(8,128)(2,1)} %param.21) | copy-start | bytes 3145732
  53.5 29.9 %all-to-all-start.5 = ((bf16[16,2,16384]{2,1,0:T(2,128)(2,1)}), bf16[16,2,16384]{2,1,0:T(2,128)(2,1)}, u32[]{:S(2)}, u32[]{:S(2)}) async-start(bf16[16,2,16384]{2,1,0:T(2,128)(2,1)} %reshape.359), calls=%async_computation.5 | async-start | bytes 2097152 | tf_op jit(solution)/shard_map/all_to_all | solution.py:110
  60.4 240.1 %all-gather.7.cloned.1.call-start = ((), (), s32[]{:S(2)}) async-start(), calls=%async_computation.10 | async-start | bytes 3145728 | tf_op jit(solution)/shard_map/all_gather | solution.py:61
  74.0 18.1 %copy-start.6 = (bf16[2,40,2048]{2,1,0:T(8,128)(2,1)S(1)}, bf16[2,40,2048]{2,1,0:T(8,128)(2,1)}, u32[]{:S(2)}) copy-start(bf16[2,40,2048]{2,1,0:T(8,128)(2,1)} %param.14) | copy-start | bytes 983044
  74.0 18.3 %copy-start.12 = (f32[2048]{0:T(1024)S(1)}, f32[2048]{0:T(1024)}, u32[]{:S(2)}) copy-start(f32[2048]{0:T(1024)} %param.17) | copy-start | bytes 24580
  83.4 30.2 %all-to-all-start.7 = ((bf16[16,2,16384]{2,1,0:T(2,128)(2,1)}), bf16[16,2,16384]{2,1,0:T(2,128)(2,1)S(1)}, u32[]{:S(2)}, u32[]{:S(2)}) async-start(bf16[16,2,16384]{2,1,0:T(2,128)(2,1)} %reshape.355), calls=%async_computation.7 | async-start | bytes 2097152 | tf_op jit(solution)/shard_map/all_to_all | solution.py:111
  113.6 1.0 copy-start.4
  114.6 48.1 %all-to-all-start.2 = ((bf16[16,30,2048]{2,1,0:T(8,128)(2,1)}), bf16[16,30,2048]{2,1,0:T(8,128)(2,1)}, u32[]{:S(2)}, u32[]{:S(2)}) async-start(bf16[16,30,2048]{2,1,0:T(8,128)(2,1)} %reshape.264), calls=%async_computation.2 | async-start | bytes 4194304 | tf_op jit(solution)/shard_map/all_to_all | solution.py:132
  121.5 182.7 %all-gather.11.cloned.1.call-start = ((), (), s32[]{:S(2)}) async-start(), calls=%async_computation.12 | async-start | bytes 3145728 | tf_op jit(solution)/shard_map/all_gather | solution.py:73
  162.7 52.4 %all-to-all-start = ((bf16[16,30,2048]{2,1,0:T(8,128)(2,1)}), bf16[16,30,2048]{2,1,0:T(8,128)(2,1)}, u32[]{:S(2)}, u32[]{:S(2)}) async-start(bf16[16,30,2048]{2,1,0:T(8,128)(2,1)} %reshape.258), calls=%async_computation | async-start | bytes 4194304 | tf_op jit(solution)/shard_map/all_to_all | solution.py:132
  215.1 34.2 %all-to-all-start.4 = ((bf16[16,1,1024,32]{2,3,1,0:T(8,128)(2,1)}), bf16[16,1,1024,32]{2,3,1,0:T(8,128)(2,1)S(1)}, u32[]{:S(2)}, u32[]{:S(2)}) async-start(bf16[16,1,1024,32]{2,3,1,0:T(8,128)(2,1)} %fusion.38), calls=%async_computation.4 | async-start | bytes 2097152 | tf_op jit(solution)/shard_map/all_to_all | solution.py:7
  226.3 77.9 %all-gather.9.cloned.1.call-start = ((), (), s32[]{:S(2)}) async-start(), calls=%async_computation.11 | async-start | bytes 3145728 | tf_op jit(solution)/shard_map/all_gather | solution.py:66
  240.3 16.5 %copy-start.5 = (bf16[16,2,16384]{2,1,0:T(2,128)(2,1)S(1)}, bf16[16,2,16384]{2,1,0:T(2,128)(2,1)}, u32[]{:S(2)}) copy-start(bf16[16,2,16384]{2,1,0:T(2,128)(2,1)} %copy-done.4) | copy-start | bytes 3145732
  249.3 7.1 %copy-start = (bf16[16,1,1024,32]{2,3,1,0:T(8,128)(2,1)}, bf16[16,1,1024,32]{2,3,1,0:T(8,128)(2,1)S(1)}, u32[]{:S(2)}) copy-start(bf16[16,1,1024,32]{2,3,1,0:T(8,128)(2,1)S(1)} %all-to-all-done.4) | copy-start | bytes 3145732
  249.3 34.8 %all-to-all-start.6 = ((bf16[16,2,16384]{2,1,0:T(2,128)(2,1)}), bf16[16,2,16384]{2,1,0:T(2,128)(2,1)}, u32[]{:S(2)}, u32[]{:S(2)}) async-start(bf16[16,2,16384]{2,1,0:T(2,128)(2,1)} %reshape.361), calls=%async_computation.6 | async-start | bytes 2097152 | tf_op jit(solution)/shard_map/all_to_all | solution.py:118
  256.2 70.9 %all-gather.13.cloned.1.call-start = ((), (), s32[]{:S(2)}) async-start(), calls=%async_computation.13 | async-start | bytes 3145728 | tf_op jit(solution)/shard_map/all_gather | solution.py:61
  284.1 29.3 %all-to-all-start.8 = ((bf16[16,2,16384]{2,1,0:T(2,128)(2,1)}), bf16[16,2,16384]{2,1,0:T(2,128)(2,1)S(1)}, u32[]{:S(2)}, u32[]{:S(2)}) async-start(bf16[16,2,16384]{2,1,0:T(2,128)(2,1)} %reshape.357), calls=%async_computation.8 | async-start | bytes 2097152 | tf_op jit(solution)/shard_map/all_to_all | solution.py:119
  290.0 43.2 %all-gather.15.cloned.1.call-start = ((), (), s32[]{:S(2)}) async-start(), calls=%async_computation.14 | async-start | bytes 3145728 | tf_op jit(solution)/shard_map/all_gather | solution.py:66
  313.4 63.7 %all-to-all-start.1 = ((bf16[16,30,2048]{2,1,0:T(8,128)(2,1)}), bf16[16,30,2048]{2,1,0:T(8,128)(2,1)}, u32[]{:S(2)}, u32[]{:S(2)}) async-start(bf16[16,30,2048]{2,1,0:T(8,128)(2,1)} %reshape.260), calls=%async_computation.1 | async-start | bytes 4194304 | tf_op jit(solution)/shard_map/all_to_all | solution.py:134
  319.9 48.5 %all-gather.17.cloned.1.call-start = ((), (), s32[]{:S(2)}) async-start(), calls=%async_computation.15 | async-start | bytes 3145728 | tf_op jit(solution)/shard_map/all_gather | solution.py:73
  377.0 7.2 %copy-start.11 = (f32[2,40,8]{1,2,0:T(8,128)S(1)}, f32[2,40,8]{1,2,0:T(8,128)}, u32[]{:S(2)}) copy-start(f32[2,40,8]{1,2,0:T(8,128)} %param.16) | copy-start | bytes 7684
  377.1 7.7 %copy-start.13 = (s32[2,1,4]{2,1,0:T(1,128)S(1)}, s32[2,1,4]{2,1,0:T(1,128)}, u32[]{:S(2)}) copy-start(s32[2,1,4]{2,1,0:T(1,128)} %param.24) | copy-start | bytes 100
  377.1 47.1 %all-to-all-start.9 = ((bf16[16,30,2048]{2,1,0:T(8,128)(2,1)}), bf16[16,30,2048]{2,1,0:T(8,128)(2,1)}, u32[]{:S(2)}, u32[]{:S(2)}) async-start(bf16[16,30,2048]{2,1,0:T(8,128)(2,1)} %reshape.273), calls=%async_computation.9 | async-start | bytes 4194304 | tf_op jit(solution)/shard_map/all_to_all | solution.py:134
  428.4 1.3 copy-start.7
  428.4 74.6 %copy-start.9 = (f32[2048]{0:T(1024)S(1)}, f32[2048]{0:T(1024)}, u32[]{:S(2)}) copy-start(f32[2048]{0:T(1024)} %param.18) | copy-start | bytes 24580
  430.8 76.2 %copy-start.8 = (bf16[2,40,2048]{2,1,0:T(8,128)(2,1)}, bf16[2,40,2048]{2,1,0:T(8,128)(2,1)S(1)}, u32[]{:S(2)}) copy-start(bf16[2,40,2048]{2,1,0:T(8,128)(2,1)S(1)} %pad_maximum_fusion) | copy-start | bytes 983044
  503.1 41.1 %copy-start.1 = (bf16[16,1,1024,32]{2,3,1,0:T(8,128)(2,1)S(1)}, bf16[16,1,1024,32]{2,3,1,0:T(8,128)(2,1)}, u32[]{:S(2)}) copy-start(bf16[16,1,1024,32]{2,3,1,0:T(8,128)(2,1)} %copy-done) | copy-start | bytes 3145732
Sparse Core Ops, SparseCore 0:
  62.8 34.3 all-gather.6
  123.9 34.3 all-gather.10
  228.7 34.4 all-gather.8
  264.6 33.1 all-gather.12
  299.7 33.5 all-gather.14
  335.2 33.1 all-gather.16
